TPU v7x, 32 devices: a whole 2x2x4 slice. The times are simulated.
32 devices in a mesh: seq: 4 (over y, x), exp: 8 (over z, core).
Axes of the slice: x: 2, y: 2, z: 4, core: 2. Of those that a mesh axis runs over, the one named last changes fastest.
Arguments:
- tokens: bfloat16 [8, 1024, 1024], P('exp', 'seq'), may hold values from -6 to 6
- lengths: int32 [8, 3], P('exp'), may hold values from 32 to 960, as said below
- expert_ids: int32 [8, 1024, 1], P('exp', 'seq'), may hold values from 0 to 7; in each aligned block of 256 rows (0 to 255, 256 to 511, ..., all dimensions but the last counted through in order) at most 64 rows name the same one
- ln1_gain: bfloat16 [1024], replicated, may hold values from 0.5 to 1.5
- ln1_bias: bfloat16 [1024], replicated, may hold values from -1.25 to 1.25
- w_query: bfloat16 [1024, 1024], replicated, may hold values from -0.25 to 0.25
- b_query: bfloat16 [1024], replicated, may hold values from -1.25 to 1.25
- w_key: bfloat16 [1024, 1024], replicated, may hold values from -0.1875 to 0.1875
- w_value: bfloat16 [1024, 1024], replicated, may hold values from -0.1875 to 0.1875
- b_value: bfloat16 [1024], replicated, may hold values from -1.25 to 1.25
- w_out: bfloat16 [1024, 1024], replicated, may hold values from -1 to 1
- b_out: bfloat16 [1024], replicated, may hold values from -1.25 to 1.25
- ln2_gain: bfloat16 [1024], replicated, may hold values from 0.5 to 1.5
- ln2_bias: bfloat16 [1024], replicated, may hold values from -1.25 to 1.25
- w_up: bfloat16 [8, 1024, 4096], P('exp', None, 'seq'), may hold values from -0.1875 to 0.1875
- b_up: bfloat16 [8, 4096], P('exp', 'seq'), may hold values from -1.25 to 1.25
- w_down: bfloat16 [8, 4096, 1024], P('exp', 'seq'), may hold values from -0.09375 to 0.09375
- b_down: bfloat16 [8, 1024], P('exp'), may hold values from -1.25 to 1.25
- cotangent: bfloat16 [8, 1024, 1024], P('exp', 'seq'), may hold values from -6 to 6
Outputs:
- output: bfloat16 [8, 1024, 1024], P('exp', 'seq')
- input_grad: float32 [8, 1024, 1024], P('exp', 'seq')
- grad_ln1_gain: float32 [1024], replicated
- grad_ln1_bias: float32 [1024], replicated
- grad_w_query: float32 [1024, 1024], replicated
- grad_b_query: float32 [1024], replicated
- grad_w_key: float32 [1024, 1024], replicated
- grad_w_value: float32 [1024, 1024], replicated
- grad_b_value: float32 [1024], replicated
- grad_w_out: float32 [1024, 1024], replicated
- grad_b_out: float32 [1024], replicated
- grad_ln2_gain: float32 [1024], replicated
- grad_ln2_bias: float32 [1024], replicated
- grad_w_up: float32 [8, 1024, 4096], P('exp', None, 'seq')
- grad_b_up: float32 [8, 4096], P('exp', 'seq')
- grad_w_down: float32 [8, 4096, 1024], P('exp', 'seq')
- grad_b_down: float32 [8, 1024], P('exp', 'seq')
Inputs may be any that keep to these rules, and one draw needn't show every extreme that they name: Each group's 3 lengths sum to 1024. `expert_ids`: among the 256 tokens of one device (aligned blocks along the token dimensions), no expert is named more than 64 times; in some blocks an expert is named exactly 64 times.
All inputs are finite; a program needn't handle non-finite values.
Results may differ from a plain program's by a relative error of at most 0.017.
Values may be sent and summed in bfloat16 or wider, within the bound.
A program may use at most 192 MiB of HBM per device.

v0:
```python
import functools
import math

import jax
import jax.numpy as jnp
from jax import lax
from jax.experimental import pallas as pl
from jax.experimental.pallas import tpu as pltpu
from jax.sharding import PartitionSpec as P

MESH = pl.DeviceIdType.MESH
F32 = jnp.float32
BF16 = jnp.bfloat16
VMEM_LIMIT = 63 * 2**20


def dot(a, b, dims=((1,), (0,))):
    return lax.dot_general(a, b, (dims, ((), ())), preferred_element_type=F32)


class Place:
    def __init__(self, n_exp):
        self.n_exp = n_exp
        self.s = lax.axis_index("seq")
        self.e = lax.axis_index("exp")
        low = lax.rem(self.s, 2)
        high = lax.div(self.s, 2)
        self.near = high * 2 + (1 - low)
        self.far = (1 - high) * 2 + low
        self.diag = (1 - high) * 2 + (1 - low)
        self.core = lax.rem(self.e, 2)
        self.chip = lax.div(self.e, 2)

    def peer(self, step, way):
        chips = self.n_exp // 2
        hop = lax.div(step, 2)
        if chips == 4:
            hop = hop + lax.div(hop, 2) * (5 - 2 * hop)
        chip = lax.rem(self.chip + way * hop + chips, chips)
        return chip * 2 + lax.rem(self.core + step, 2)

    def greet(self, diag=False):
        barrier = pltpu.get_barrier_semaphore()
        others = (self.near, self.far, self.diag) if diag else (self.near, self.far)
        for other in others:
            pl.semaphore_signal(barrier, inc=1, device_id=(other, self.e), device_id_type=MESH)

        def tell(step, carry):
            pl.semaphore_signal(
                barrier, inc=1, device_id=(self.s, self.peer(step, 1)), device_id_type=MESH
            )
            return carry

        lax.fori_loop(1, self.n_exp, tell, 0)
        pl.semaphore_wait(barrier, len(others) + self.n_exp - 1)

    def to_seq(self, src, dst, send_sem, recv_sem, other):
        return pltpu.make_async_remote_copy(
            src_ref=src, dst_ref=dst, send_sem=send_sem, recv_sem=recv_sem,
            device_id=(other, self.e), device_id_type=MESH,
        )

    def to_exp(self, src, dst, send_sem, recv_sem, other):
        return pltpu.make_async_remote_copy(
            src_ref=src, dst_ref=dst, send_sem=send_sem, recv_sem=recv_sem,
            device_id=(self.s, other), device_id_type=MESH,
        )


class Dispatch:
    def __init__(self, place, send, held, exp_sems, seq_sems):
        self.place, self.send, self.held = place, send, held
        self.exp_send, self.exp_recv = exp_sems
        self.seq_send, self.seq_recv = seq_sems
        self.cap = send.shape[1]

    @staticmethod
    def scratch(n_exp):
        return [
            pltpu.SemaphoreType.DMA((n_exp,)),
            pltpu.SemaphoreType.DMA((n_exp,)),
            pltpu.SemaphoreType.DMA((n_exp, 6)),
            pltpu.SemaphoreType.DMA((n_exp, 6)),
        ]

    def _exp(self, step):
        p = self.place
        other = p.peer(step, -1)
        return p.to_exp(
            self.send.at[other], self.held.at[step, p.s], self.exp_send.at[step], self.exp_recv.at[step], other
        )

    def _seq(self, step, owner, half, lane, other):
        p = self.place
        rows = pl.ds(half * (self.cap // 2), self.cap // 2)
        part = self.held.at[step, owner, rows]
        return p.to_seq(part, part, self.seq_send.at[step, lane], self.seq_recv.at[step, lane], other)

    def copies(self, step, lanes=range(6)):
        p = self.place
        spec = (
            (p.s, 0, p.near),
            (p.s, 1, p.far),
            (p.s, 1, p.near),
            (p.s, 0, p.far),
            (p.near, 0, p.far),
            (p.far, 1, p.near),
        )
        return [self._seq(step, spec[n][0], spec[n][1], n, spec[n][2]) for n in lanes]

    def start_exp(self, step):
        self._exp(step).start()

    def own(self):
        p = self.place
        self.held[0, p.s] = self.send[p.e]

    def start_seq(self, step):
        @pl.when(step > 0)
        def _():
            self._exp(step).wait_recv()

        for c in self.copies(step, range(4)):
            c.start()

    def relay(self, step):
        for c, out in zip(self.copies(step, (0, 1)), self.copies(step, (4, 5))):
            c.wait_recv()
            out.start()

    def arrived(self, step):
        for c in self.copies(step, range(2, 6)):
            c.wait_recv()

    def sent(self, step):
        for c in self.copies(step):
            c.wait_send()

    def drain(self, seq=True):
        def body(step, carry):
            if seq:
                self.sent(step)

            @pl.when(step > 0)
            def _():
                self._exp(step).wait_send()

            return carry

        lax.fori_loop(0, self.place.n_exp, body, 0)


class Combine:
    def __init__(self, place, part, passing, landing, total, back, seq_sems, exp_sems, slots):
        self.place, self.part, self.passing, self.landing = place, part, passing, landing
        self.total, self.back, self.slots = total, back, slots
        self.seq_send, self.seq_recv = seq_sems
        self.exp_send, self.exp_recv = exp_sems
        self.half = part.shape[2] // 2

    @staticmethod
    def scratch(n_exp, cap, width):
        return [
            pltpu.VMEM((n_exp, 2, cap // 2, width), BF16),
            pltpu.VMEM((n_exp, 4, cap // 2, width), BF16),
            pltpu.VMEM((n_exp, cap, width), BF16),
            pltpu.SemaphoreType.DMA((n_exp, 6)),
            pltpu.SemaphoreType.DMA((n_exp, 6)),
            pltpu.SemaphoreType.DMA((n_exp,)),
            pltpu.SemaphoreType.DMA((n_exp,)),
        ]

    def _slot(self, step):
        return lax.rem(step, self.slots)

    def _piece(self, step, owner, half):
        return self.part.at[self._slot(step), owner, pl.ds(half * self.half, self.half)]

    def _seq(self, src, dst, step, lane, other):
        return self.place.to_seq(
            src, dst, self.seq_send.at[step, lane], self.seq_recv.at[step, lane], other
        )

    def copies(self, step, lanes=range(6)):
        p = self.place
        spec = (
            (p.diag, 0, self.passing, 0, p.near),
            (p.diag, 1, self.passing, 1, p.far),
            (p.near, 0, self.landing, 0, p.near),
            (p.far, 1, self.landing, 3, p.far),
            (p.far, 0, self.landing, 2, p.far),
            (p.near, 1, self.landing, 1, p.near),
        )
        made = []
        for n in lanes:
            owner, half, buffer, at, other = spec[n]
            made.append(self._seq(self._piece(step, owner, half), buffer.at[step, at], step, n, other))
        return made

    def start(self, step):
        for c in self.copies(step, range(4)):
            c.start()

    def pass_on(self, step):
        p = self.place
        slot = self._slot(step)
        came, out = self.copies(step, (0, 1)), self.copies(step, (4, 5))
        for n, owner in enumerate((p.far, p.near)):
            rows = pl.ds(n * self.half, self.half)
            came[n].wait_recv()
            self.part[slot, owner, rows] = (
                self.part[slot, owner, rows].astype(F32) + self.passing[step, n].astype(F32)
            ).astype(BF16)
            out[n].start()

    def _whole(self, step):
        if self.total is None:
            return self.part.at[self._slot(step), self.place.s]
        return self.total.at[step]

    def _exp(self, step):
        p = self.place
        other = p.peer(step, 1)
        return p.to_exp(
            self._whole(step), self.back.at[p.e], self.exp_send.at[step], self.exp_recv.at[step], other
        )

    def arrived(self, step):
        copies = self.copies(step)
        for c in copies[2:]:
            c.wait_recv()
        for c in copies:
            c.wait_send()

    def summed(self, step, half):
        rows = pl.ds(half * self.half, self.half)
        return (
            self.part[self._slot(step), self.place.s, rows].astype(F32)
            + self.landing[step, half].astype(F32)
            + self.landing[step, 2 + half].astype(F32)
        )

    def finish(self, step, bias=None):
        p = self.place
        self.arrived(step)
        for half in range(2):
            value = self.summed(step, half)
            if bias is not None:
                value = value + bias
            rows = pl.ds(half * self.half, self.half)
            if self.total is None:
                self.part[self._slot(step), p.s, rows] = value.astype(BF16)
            else:
                self.total[step, rows] = value.astype(BF16)

        @pl.when(step > 0)
        def _():
            self._exp(step).start()

        @pl.when(step == 0)
        def _():
            self.back[p.e] = self._whole(0)[...]

    def drain(self):
        p = self.place

        def body(step, carry):
            c = self._exp(step)
            c.wait_send()
            c.wait_recv()
            return carry

        lax.fori_loop(1, p.n_exp, body, 0)


GELU_A = math.sqrt(2.0 / math.pi)
GELU_B = 0.044715


EPSILON = 1e-05
SCORE_SCALE = 0.125
MASKED_SCORE = -1e30
HEAD_DIM = 64
HEADS = 16


class Gather:
    def __init__(self, place, held, send_sems, recv_sems):
        self.place, self.held = place, held
        self.send_sems, self.recv_sems = send_sems, recv_sems
        self.half = held.shape[1] // 2

    @staticmethod
    def scratch():
        return [pltpu.SemaphoreType.DMA((6,)), pltpu.SemaphoreType.DMA((6,))]

    def copies(self, lanes=range(6)):
        p = self.place
        spec = (
            (p.s, 0, p.near),
            (p.s, 1, p.far),
            (p.s, 1, p.near),
            (p.s, 0, p.far),
            (p.near, 0, p.far),
            (p.far, 1, p.near),
        )
        made = []
        for n in lanes:
            owner, half, other = spec[n]
            part = self.held.at[owner, pl.ds(half * self.half, self.half)]
            made.append(p.to_seq(part, part, self.send_sems.at[n], self.recv_sems.at[n], other))
        return made

    def start(self):
        for c in self.copies(range(4)):
            c.start()

    def relay(self):
        for c, out in zip(self.copies((0, 1)), self.copies((4, 5))):
            c.wait_recv()
            out.start()

    def wait(self, lanes):
        for c in self.copies(lanes):
            c.wait_recv()

    def drain(self):
        for c in self.copies():
            c.wait_send()


def layer_norm(values, gain, shift):
    center = values - jnp.mean(values, axis=-1, keepdims=True)
    inv_std = lax.rsqrt(jnp.mean(center * center, axis=-1, keepdims=True) + EPSILON)
    xhat = center * inv_std
    return xhat * gain + shift, xhat, inv_std


def norm_back(grad, xhat, inv_std, gain):
    d = grad * gain
    return (
        d - jnp.mean(d, axis=-1, keepdims=True) - xhat * jnp.mean(d * xhat, axis=-1, keepdims=True)
    ) * inv_std


def row_choice(ids, n_exp, cap):
    tokens = ids.shape[1]
    named = (ids == lax.broadcasted_iota(jnp.int32, (128, tokens), 0)).astype(BF16)
    before = (
        lax.broadcasted_iota(jnp.int32, (tokens, tokens), 0)
        < lax.broadcasted_iota(jnp.int32, (tokens, tokens), 1)
    ).astype(BF16)
    earlier = dot(named, before) * named.astype(F32)
    slot = jnp.sum(earlier, axis=0, keepdims=True).astype(jnp.int32) + ids * cap
    return (slot == lax.broadcasted_iota(jnp.int32, (n_exp * cap, tokens), 0)).astype(BF16)


def segment_of(position, lengths):
    end = jnp.int32(0)
    count = jnp.zeros_like(position)
    for n in range(lengths.shape[1]):
        end = end + lengths[0, n]
        count = count + (position >= end).astype(jnp.int32)
    return count


def head_mask(rows, width, head):
    lane = lax.broadcasted_iota(jnp.int32, (rows, width), 1)
    return (lane >= head * HEAD_DIM) & (lane < (head + 1) * HEAD_DIM)


class SumAll:
    def __init__(self, place, src, core_in, mine, chip_in, res, where, local_sem, sems):
        self.place, self.src, self.core_in, self.mine = place, src, core_in, mine
        self.chip_in, self.res, self.where, self.local_sem = chip_in, res, where, local_sem
        (self.core_sems, self.rs_send, self.rs_recv, self.ag_send, self.ag_recv,
         self.seq_send, self.seq_recv, self.pair_send, self.pair_recv) = sems
        self.chips = place.n_exp // 2
        p = place
        self.sibling = p.chip * 2 + (1 - p.core)

    @staticmethod
    def scratch(n_exp, *piece):
        chips = n_exp // 2
        dma = pltpu.SemaphoreType.DMA
        return [
            pltpu.VMEM((2, chips, *piece), BF16),
            pltpu.VMEM((chips, *piece), BF16),
            pltpu.VMEM((chips, *piece), BF16),
            pltpu.VMEM((chips, *piece), BF16),
            pltpu.VMEM(piece, BF16),
            dma((1,)),
            dma((2,)),
            dma((chips,)),
            dma((chips,)),
            dma((chips,)),
            dma((chips,)),
            dma((chips, 6)),
            dma((chips, 6)),
            dma((chips, 4)),
            dma((chips, 4)),
        ]

    def chip(self, hop):
        return lax.rem(self.place.chip + hop, self.chips)

    def exp(self, hop):
        return self.chip(hop) * 2 + self.place.core

    def _core(self):
        p = self.place
        return p.to_exp(
            self.src.at[1 - p.core], self.core_in, self.core_sems.at[0], self.core_sems.at[1], self.sibling
        )

    def start(self):
        self._core().start()

    def _spread(self, hop):
        p = self.place
        to = self.chip(hop)
        return p.to_exp(
            self.mine.at[to], self.chip_in.at[p.chip], self.rs_send.at[to], self.rs_recv.at[p.chip], self.exp(hop)
        )

    def _spread_from(self, hop):
        p = self.place
        at = self.chip(hop)
        return p.to_exp(
            self.mine.at[at], self.chip_in.at[at], self.rs_send.at[at], self.rs_recv.at[at], self.exp(hop)
        )

    def spread(self):
        p = self.place
        self._core().wait_recv()
        for n in range(self.chips):
            self.mine[n] = (self.src[p.core, n].astype(F32) + self.core_in[n].astype(F32)).astype(BF16)
        for hop in range(1, self.chips):
            self._spread(hop).start()

    def _local(self):
        p = self.place
        return pltpu.make_async_copy(self.res, self.where(p.s, p.e), self.local_sem.at[0])

    def _share(self, hop):
        p = self.place
        to = self.chip(hop)
        return p.to_exp(
            self.res, self.where(p.s, p.e), self.ag_send.at[to], self.ag_recv.at[p.chip], self.exp(hop)
        )

    def _share_from(self, hop):
        p = self.place
        at = self.chip(hop)
        return p.to_exp(
            self.res, self.where(p.s, self.exp(hop)), self.ag_send.at[at], self.ag_recv.at[at], self.exp(hop)
        )

    def copies(self, hop, lanes=range(6)):
        p = self.place
        spec = (
            (p.s, 0, p.near),
            (p.s, 1, p.far),
            (p.s, 1, p.near),
            (p.s, 0, p.far),
            (p.near, 0, p.far),
            (p.far, 1, p.near),
        )
        made = []
        for n in lanes:
            owner, half, other = spec[n]
            part = self.where(owner, self.exp(hop), half)
            made.append(p.to_seq(part, part, self.seq_send.at[hop, n], self.seq_recv.at[hop, n], other))
        return made

    def _pair(self, hop, n):
        p = self.place
        part = self.where((p.s, p.near, p.far, p.diag)[n], self.exp(hop))
        return p.to_exp(part, part, self.pair_send.at[hop, n], self.pair_recv.at[hop, n], self.sibling)

    def _pair_from(self, hop, n):
        p = self.place
        owner = (p.s, p.near, p.far, p.diag)[n]
        part = self.where(owner, self.chip(hop) * 2 + (1 - p.core))
        return p.to_exp(part, part, self.pair_send.at[hop, n], self.pair_recv.at[hop, n], self.sibling)

    def reduce(self):
        p = self.place
        for hop in range(1, self.chips):
            self._spread_from(hop).wait_recv()
        total = self.mine[p.chip].astype(F32)
        for hop in range(1, self.chips):
            total = total + self.chip_in[self.chip(hop)].astype(F32)
        self.res[...] = total.astype(BF16)
        self._local().start()
        for hop in range(1, self.chips):
            self._share(hop).start()
        self._local().wait()

    def forward(self, hop):
        if hop > 0:
            self._share_from(hop).wait_recv()
        for c in self.copies(hop, range(4)):
            c.start()
        self._pair(hop, 0).start()

    def relay(self, hop):
        for c, out in zip(self.copies(hop, (0, 1)), self.copies(hop, (4, 5))):
            c.wait_recv()
            out.start()

    def arrived(self, hop):
        for c in self.copies(hop, (2, 3)):
            c.wait_recv()
        self._pair(hop, 1).start()
        self._pair(hop, 2).start()
        for c in self.copies(hop, (4, 5)):
            c.wait_recv()
        self._pair(hop, 3).start()

    def drain(self):
        self._core().wait_send()
        for hop in range(1, self.chips):
            self._spread(hop).wait_send()
            self._share(hop).wait_send()
        for hop in range(self.chips):
            for c in self.copies(hop):
                c.wait_send()
            for n in range(4):
                self._pair(hop, n).wait_send()
                self._pair_from(hop, n).wait_recv()


def layer(
    tokens, ids, cotangent, lengths, ln1, w_qkv, b_query, b_value, w_out, b_out, ln2, w_up, b_up, w_down, b_down,
    n_exp, collective_id,
):
    tok, width = tokens.shape
    hidden = w_up.shape[1]
    n_seq = 4
    total = n_seq * tok
    cols = width // n_seq
    heads = cols // HEAD_DIM
    cap = 2 * tok // n_exp
    q_block = 256
    chips = n_exp // 2
    rows_w, rows_o = width // n_exp, cols // n_exp
    pairs = cols // 128
    per_pair = 128 // HEAD_DIM
    routed = n_seq * cap
    block = min(256, hidden)
    slots = 2
    ahead = 5

    vm = pltpu.VMEM
    dma = pltpu.SemaphoreType.DMA
    table = dict(
        xall=vm((1, n_seq, tok, width), BF16),
        n1=vm((width, total), BF16),
        q=vm((total, cols), BF16),
        k=vm((total, cols), BF16),
        v=vm((total, cols), BF16),
        attn=vm((total, cols), F32),
        lse=vm((8, total), F32),
        resid=vm((tok, width), F32),
        pick=vm((n_exp * cap, tok), BF16),
        w_all=vm((width, 3 * cols), BF16),
        w_o=vm((width, width), BF16),
        send_c=vm((n_exp, cap, width), BF16),
        send_n=vm((n_exp, cap, width), BF16),
        back=vm((n_exp, cap, width), BF16),
        ret=vm((n_exp, cap, width), BF16),
        attn_out=vm((n_seq, tok, cols), BF16),
        attn_in=vm((n_seq, tok, cols), BF16),
        cot=vm((n_exp, n_seq, cap, width), BF16),
        held=vm((n_exp, n_seq, cap, width), BF16),
        wu=vm((width, hidden), BF16),
        wd=vm((hidden, width), BF16),
        part=vm((slots, n_seq, cap, width), BF16),
        dwu=vm((width, hidden), F32),
        dwd=vm((hidden, width), F32),
        dqkv=vm((total, 3 * cols), BF16),
        vec_own=vm((8, width), F32),
        vec_seq=vm((n_seq, 8, width), F32),
        vec_exp=vm((n_exp, 8, width), F32),
        local_sems=dma((8,)),
        load_sems=dma((3 * pairs,)),
        dq=vm((tok, cols), F32),
        a2a_send=dma((n_seq,)),
        a2a_recv=dma((n_seq,)),
        vs_send=dma((n_seq,)),
        vs_recv=dma((n_seq,)),
        ve_send=dma((n_exp,)),
        ve_recv=dma((n_exp,)),
    )
    groups = dict(
        gather1=Gather.scratch(),
        gather2=Gather.scratch(),
        disp_c=Dispatch.scratch(n_exp),
        disp_n=Dispatch.scratch(n_exp),
        comb_g=Combine.scratch(n_exp, cap, width),
        comb_f=Combine.scratch(n_exp, cap, width)[:2] + Combine.scratch(n_exp, cap, width)[3:],
        red=[
            vm((1, 2, tok // 2, width), BF16),
            vm((1, 4, tok // 2, width), BF16),
            dma((1, 6)),
            dma((1, 6)),
        ],
        sum_o=SumAll.scratch(n_exp, rows_o, width),
        **{f"sum_{j}": SumAll.scratch(n_exp, 3, rows_w, 128) for j in range(pairs)},
    )
    scratch = list(table.values()) + [ref for group in groups.values() for ref in group]

    def kernel(tok_ref, ids_ref, cot_ref, len_ref, g1_ref, c1_ref, wq_in, wk_in, wv_in, bq_ref, bv_ref, wo_in, bo_ref,
               g2_ref, c2_ref, wu_in, bu_ref, wd_in, bd_ref,
               out_out, gin_out, vec_ref, dbu_ref, csum_ref, dwu_out, dwd_out, gw_out, go_out, *refs):
        r = dict(zip(table, refs))
        at = len(table)
        g = {}
        for name, group in groups.items():
            g[name] = refs[at : at + len(group)]
            at += len(group)
        xall, n1, q_all, k_all, v_all = r["xall"], r["n1"], r["q"], r["k"], r["v"]
        attn, lse_all, resid, pick = r["attn"], r["lse"], r["resid"], r["pick"]
        w_all, w_o, wu, wd = r["w_all"], r["w_o"], r["wu"], r["wd"]
        send_c, send_n, back, ret = r["send_c"], r["send_n"], r["back"], r["ret"]
        attn_out, attn_in, cot, held, part = r["attn_out"], r["attn_in"], r["cot"], r["held"], r["part"]
        dwu, dwd, dqkv = r["dwu"], r["dwd"], r["dqkv"]
        gattn = attn_out
        gin_ref = dwd.at[0:tok, :]
        dk, dv = dwu.at[0:total, 0:cols], dwu.at[0:total, cols : 2 * cols]
        vec_own, vec_seq, vec_exp = r["vec_own"], r["vec_seq"], r["vec_exp"]
        local_sems, load_sems, dq = r["local_sems"], r["load_sems"], r["dq"]

        p = Place(n_exp)
        mine = pl.ds(pl.multiple_of(p.s * cols, cols), cols)

        tile = 32

        def tile_rows(n):
            return pl.ds(pl.multiple_of(n * tile, tile), tile)

        def row_of(ref):
            return ref[...].astype(F32).reshape(1, ref.shape[-1])

        loads = [
            pltpu.make_async_copy(
                src.at[:, pl.ds(pl.multiple_of(p.s * cols + j * 128, 128), 128)],
                w_all.at[:, pl.ds((3 * j + m) * 128, 128)],
                load_sems.at[3 * j + m],
            )
            for m, src in enumerate((wq_in, wk_in, wv_in))
            for j in range(pairs)
        ]
        load_o = pltpu.make_async_copy(wo_in, w_o, local_sems.at[3])
        load_ffn = [
            pltpu.make_async_copy(wu_in, wu, local_sems.at[4]),
            pltpu.make_async_copy(wd_in, wd, local_sems.at[5]),
        ]
        for c in loads + [load_o] + load_ffn:
            c.start()

        xall[0, p.s] = tok_ref[...]
        p.greet(diag=True)
        gather1 = Gather(p, xall.at[0], *g["gather1"])
        gather1.start()
        pick[...] = row_choice(ids_ref[...], n_exp, cap)

        def lay_out(send, rows_ref):
            for e in range(0, n_exp, 2):
                laid = dot(pick[e * cap : (e + 2) * cap, :], rows_ref[...])
                send[e : e + 2] = laid.astype(BF16).reshape(2, cap, width)

        lay_out(send_c, cot_ref)
        disp_c = Dispatch(p, send_c, cot, g["disp_c"][0:2], g["disp_c"][2:4])
        for step in range(1, n_exp):
            disp_c.start_exp(step)
        disp_c.own()
        gain1, bias1 = row_of(g1_ref), row_of(c1_ref)
        gain2, bias2 = row_of(g2_ref), row_of(c2_ref)
        bq = bq_ref[mine].astype(F32).reshape(1, cols)
        bv = bv_ref[mine].astype(F32).reshape(1, cols)

        def project(owner):
            rows = pl.ds(pl.multiple_of(owner * tok, tok), tok)

            def norm_tile(n, carry):
                x = xall[0, owner, tile_rows(n), :].astype(F32)
                per = cap // tile
                rows = pl.ds(pl.multiple_of(lax.rem(n, per) * tile, tile), tile)
                part[0, lax.div(n, per), rows, :] = layer_norm(x, gain1, bias1)[0].astype(BF16)
                return carry

            lax.fori_loop(0, tok // tile, norm_tile, 0)
            normed = part[0].reshape(tok, width)
            n1[:, rows] = jnp.transpose(normed)
            out = dot(normed, w_all[...])
            for j in range(pairs):
                at, first = slice(j * 128, (j + 1) * 128), 3 * j * 128
                q = (out[:, first : first + 128] + bq[:, at]).astype(BF16)
                q_all[rows, at] = (q.astype(F32) * SCORE_SCALE).astype(BF16)
                k_all[rows, at] = out[:, first + 128 : first + 256].astype(BF16)
                v_all[rows, at] = (out[:, first + 256 : first + 384] + bv[:, at]).astype(BF16)

        for c in loads:
            c.wait()
        project(p.s)
        gather1.relay()
        gather1.wait((2, 3))
        project(p.near)
        project(p.far)
        gather1.wait((4, 5))
        disp_c.start_seq(0)
        disp_c.start_seq(1)
        project(p.diag)

        def a2a(owner):
            return p.to_seq(
                attn_out.at[owner], attn_in.at[p.s], r["a2a_send"].at[owner], r["a2a_recv"].at[p.s], owner
            )

        def a2a_from(owner):
            return p.to_seq(
                attn_out.at[owner], attn_in.at[owner], r["a2a_send"].at[owner], r["a2a_recv"].at[owner], owner
            )

        blocks = total // q_block
        for n in reversed(range(blocks)):
            seen = (n + 1) * q_block
            rows = pl.ds(n * q_block, q_block)
            q_pos = lax.broadcasted_iota(jnp.int32, (q_block, 1), 0) + n * q_block
            k_pos = lax.broadcasted_iota(jnp.int32, (1, seen), 1)
            allowed = (segment_of(q_pos, len_ref) == segment_of(k_pos, len_ref)) & (k_pos <= q_pos)
            q_rows = q_all[rows, :]
            acc = jnp.zeros((q_block, cols), F32)
            lse = jnp.zeros((q_block, 128), F32)
            lane = lax.broadcasted_iota(jnp.int32, (q_block, 128), 1)
            for head in range(heads):
                own = head_mask(q_block, cols, head)
                scores = dot(jnp.where(own, q_rows, jnp.zeros_like(q_rows)), k_all[0:seen, :], ((1,), (1,)))
                scores = jnp.where(allowed, scores, MASKED_SCORE)
                top = jnp.max(scores, axis=1, keepdims=True)
                weights = jnp.exp(scores - top)
                sums = jnp.sum(weights, axis=1, keepdims=True)
                out = dot(weights.astype(BF16), v_all[0:seen, :]) / sums
                acc = jnp.where(own, out, acc)
                lse = jnp.where(lane == head, top + jnp.log(sums), lse)
            attn[rows, :] = acc
            lse_all[:, rows] = jnp.transpose(lse)[0:8, :]
            owner, first = (n * q_block) // tok, (n * q_block) % tok
            attn_out[owner, pl.ds(first, q_block)] = acc.astype(BF16)
            if first == 0:

                @pl.when(p.s != owner)
                def _(owner=owner):
                    a2a(owner).start()

                @pl.when(p.s == owner)
                def _(owner=owner):
                    attn_in[owner] = attn_out[owner]

        disp_c.start_seq(2)
        disp_c.relay(0)
        disp_c.relay(1)
        load_o.wait()
        sums = tok_ref[...].astype(F32) + row_of(bo_ref)
        for owner in range(n_seq):

            @pl.when(p.s != owner)
            def _(owner=owner):
                a2a_from(owner).wait_recv()

            sums = sums + dot(attn_in[owner], w_o[pl.ds(owner * cols, cols), :])
        resid[...] = sums
        disp_c.start_seq(3)
        disp_c.relay(2)

        gather1.drain()
        for owner in range(n_seq):

            @pl.when(p.s != owner)
            def _(owner=owner):
                a2a(owner).wait_send()

        gout = xall.at[0]
        low = gout.at[p.s]

        def norm_two_tile(n, carry):
            low[tile_rows(n), :] = layer_norm(resid[tile_rows(n), :], gain2, bias2)[0].astype(BF16)
            return carry

        lax.fori_loop(0, tok // tile, norm_two_tile, 0)
        lay_out(send_n, low)

        disp_n = Dispatch(p, send_n, held, g["disp_n"][0:2], g["disp_n"][2:4])
        comb_g = Combine(p, part, *g["comb_g"][0:3], back, g["comb_g"][3:5], g["comb_g"][5:7], slots)
        comb_f = Combine(p, held, *g["comb_f"][0:2], None, ret, g["comb_f"][2:4], g["comb_f"][4:6], n_exp)
        disp_n.own()
        disp_n.start_seq(0)
        for step in range(1, n_exp):
            disp_n.start_exp(step)
        disp_c.start_seq(4)
        disp_c.relay(3)
        dwu[...] = jnp.zeros_like(dwu)
        dwd[...] = jnp.zeros_like(dwd)
        dbu_ref[...] = jnp.zeros_like(dbu_ref)
        csum_ref[...] = jnp.zeros_like(csum_ref)
        bias_down = bd_ref[...].astype(F32)
        for c in load_ffn:
            c.wait()

        def ffn_start(*steps):
            for step in steps:
                comb_f.start(step)

        def ffn_pass(*steps):
            for step in steps:
                comb_f.pass_on(step)

        def ffn_finish(*steps):
            for step in steps:
                comb_f.finish(step, bias_down)

        def compute(step):
            x = held[step].reshape(routed, width)
            gr = cot[step].reshape(routed, width)
            ones = jnp.ones((8, routed), BF16)
            csum_ref[...] += dot(ones, gr)[0:1, :]
            y = jnp.zeros((routed, width), F32)
            gx = jnp.zeros((routed, width), F32)
            for b in range(hidden // block):
                at = pl.ds(b * block, block)
                wu_b, wd_b = wu[:, at], wd[at, :]
                pre = dot(x, wu_b) + bu_ref[:, at].astype(F32)
                g_act = dot(gr, wd_b, ((1,), (1,)))
                sq = pre * pre
                th = jnp.tanh(GELU_A * pre * (1.0 + GELU_B * sq))
                half = 0.5 * (1.0 + th)
                act = (pre * half).astype(BF16)
                slope = half + 0.5 * pre * (1.0 - th * th) * (GELU_A * (1.0 + 3.0 * GELU_B * sq))
                g_pre = (g_act * slope).astype(BF16)
                dbu_ref[:, at] += dot(ones, g_pre)[0:1, :]
                y = y + dot(act, wd_b)
                gx = gx + dot(g_pre, wu_b, ((1,), (1,)))
                dwu[:, at] += dot(x, g_pre, ((0,), (0,)))
                dwd[at, :] += dot(act, gr, ((0,), (0,)))
            part[lax.rem(step, slots)] = gx.astype(BF16).reshape(n_seq, cap, width)
            disp_n.sent(step)
            held[step] = y.astype(BF16).reshape(n_seq, cap, width)

        stores = [
            pltpu.make_async_copy(dwu, dwu_out, local_sems.at[6]),
            pltpu.make_async_copy(dwd, dwd_out, local_sems.at[7]),
        ]

        def loop(t, carry):
            @pl.when(t + ahead - 1 < n_exp)
            def _():
                disp_c.start_seq(t + ahead - 1)

            @pl.when(t + ahead - 2 < n_exp)
            def _():
                disp_c.relay(t + ahead - 2)

            @pl.when(t <= n_exp)
            def _():
                disp_n.relay(t - 1)

            @pl.when(t < n_exp)
            def _():
                disp_n.start_seq(t)

            @pl.when((t >= 3) & (t <= n_exp + 2))
            def _():
                comb_g.pass_on(t - 3)

            @pl.when(t >= 4)
            def _():
                comb_g.finish(t - 4)

            @pl.when(t == n_exp + 1)
            def _():
                ffn_start(0)

            @pl.when((t >= 2) & (t <= n_exp + 1))
            def _():
                disp_c.arrived(t - 2)
                disp_n.arrived(t - 2)
                compute(t - 2)
                comb_g.start(t - 2)

            @pl.when(t == n_exp + 1)
            def _():
                for c in stores:
                    c.start()
                ffn_start(1)

            @pl.when(t == n_exp + 2)
            def _():
                ffn_start(2)

            @pl.when(t == n_exp + 3)
            def _():
                ffn_start(3)

            return carry

        lax.fori_loop(1, n_exp + 4, loop, 0)
        ffn_pass(0, 1)
        comb_g.drain()
        ffn_pass(2, 3)

        for c in stores:
            c.wait()
        gin_ref[...] = dot(pick[...], back[...].reshape(n_exp * cap, width), ((0,), (0,)))

        def norm_two_back(n, carry):
            at = tile_rows(n)
            g_two = gin_ref[at, :]
            _, xhat, inv_std = layer_norm(resid[at, :], gain2, 0.0)
            g_resid = cot_ref[at, :].astype(F32) + norm_back(g_two, xhat, inv_std, gain2)
            gin_ref[at, :] = g_resid
            g_low = g_resid.astype(BF16)
            gout[p.s, at, :] = g_low
            new = (g_low.astype(F32), g_two * xhat, g_two)
            return tuple(old + jnp.sum(v, axis=0, keepdims=True) for old, v in zip(carry, new))

        zero_row = jnp.zeros((1, width), F32)
        sums2 = lax.fori_loop(0, tok // tile, norm_two_back, (zero_row,) * 3)
        gather2 = Gather(p, gout, *g["gather2"])
        gather2.start()
        vec_own[...] = jnp.zeros_like(vec_own)
        for n in range(3):
            vec_own[4 + n : 5 + n, :] = sums2[n]
        wo_mine = w_o.at[mine, :]

        def grad_attn(owner):
            gattn[owner] = dot(gout[owner], wo_mine[...], ((1,), (1,))).astype(BF16)

        dwu[0:total, 0 : 2 * cols] = jnp.zeros((total, 2 * cols), F32)

        head_rows = lax.broadcasted_iota(jnp.int32, (8, cols), 0)
        head_lane = lax.broadcasted_iota(jnp.int32, (8, cols), 1)
        per_head = (lax.div(head_lane, HEAD_DIM) == head_rows).astype(F32)

        def attn_back(owner, some_heads):
            rows = pl.ds(pl.multiple_of(owner * tok, tok), tok)
            q_pos = lax.broadcasted_iota(jnp.int32, (1, tok), 1) + owner * tok
            q_seg = segment_of(q_pos, len_ref)
            q_rows, g_rows = q_all[rows, :], gattn[owner]
            delta = lax.dot_general(
                per_head, g_rows.astype(F32) * attn[rows, :], (((1,), (1,)), ((), ())),
                precision=lax.Precision.HIGHEST, preferred_element_type=F32,
            )
            dq[...] = jnp.zeros_like(dq)

            def key_block(n, carry):
                keys = pl.ds(pl.multiple_of(n * tok, tok), tok)
                k_pos = lax.broadcasted_iota(jnp.int32, (tok, 1), 0) + n * tok
                allowed = (q_seg == segment_of(k_pos, len_ref)) & (k_pos <= q_pos)
                k_rows, v_rows = k_all[keys, :], v_all[keys, :]
                dq_new = jnp.zeros((tok, cols), F32)
                dk_new = jnp.zeros((tok, cols), F32)
                dv_new = jnp.zeros((tok, cols), F32)
                for head in some_heads:
                    own = head_mask(tok, cols, head)
                    q_own = jnp.where(own, q_rows, jnp.zeros_like(q_rows))
                    g_own = jnp.where(own, g_rows, jnp.zeros_like(g_rows))
                    scores = dot(k_rows, q_own, ((1,), (1,)))
                    probs = jnp.where(allowed, jnp.exp(scores - lse_all[head : head + 1, rows]), 0.0)
                    g_probs = dot(v_rows, g_own, ((1,), (1,)))
                    g_scores = (probs * (g_probs - delta[head : head + 1, :])).astype(BF16)
                    dk_new = dk_new + dot(g_scores, q_own)
                    dv_new = dv_new + dot(probs.astype(BF16), g_own)
                    dq_new = dq_new + jnp.where(own, dot(g_scores, k_rows, ((0,), (0,))), 0.0)
                dk[keys, :] += dk_new
                dv[keys, :] += dv_new
                dq[...] += dq_new
                return carry

            lax.fori_loop(0, owner + 1, key_block, 0)
            low_dq = (dq[...] * SCORE_SCALE).astype(BF16)
            for j in sorted({head // per_pair for head in some_heads}):
                dqkv[rows, pl.ds(3 * j * 128, 128)] = low_dq[:, j * 128 : (j + 1) * 128]

        every = range(heads)
        grad_attn(p.s)
        gather2.relay()
        attn_back(p.s, every)
        ffn_finish(0, 1, 2, 3)
        gather2.wait((2, 3))
        grad_attn(p.near)
        attn_back(p.near, every)
        grad_attn(p.far)
        attn_back(p.far, every)
        gather2.wait((4, 5))
        ffn_start(4, 5, 6, 7)
        grad_attn(p.diag)

        def place_w(j, owner, e, half=None):
            rows = rows_w if half is None else rows_w // 2
            first = e * rows_w + (0 if half is None else half * rows)
            return gw_out.at[
                :, pl.ds(pl.multiple_of(first, rows), rows), pl.ds(pl.multiple_of(owner * cols + j * 128, 128), 128)
            ]

        def place_o(owner, e, half=None):
            rows = pl.ds(pl.multiple_of(owner * cols + e * rows_o, rows_o), rows_o)
            if half is None:
                return go_out.at[rows, :]
            return go_out.at[rows, pl.ds(half * (width // 2), width // 2)]

        def summing(name, place):
            return SumAll(p, *g[name][0:5], place, g[name][5], g[name][6:])

        sum_w = [summing(f"sum_{j}", functools.partial(place_w, j)) for j in range(pairs)]
        sum_o = summing("sum_o", place_o)

        for b in range(cols // 128):
            a_low = attn[:, b * 128 : (b + 1) * 128].astype(BF16)
            got = dot(a_low, gout[...].reshape(total, width), ((0,), (0,))).astype(BF16)
            for n in range(128 // rows_o):
                e = b * (128 // rows_o) + n
                sum_o.src[e % 2, e // 2] = got[n * rows_o : (n + 1) * rows_o]
        for j in range(pairs):
            attn_back(p.diag, range(j * per_pair, (j + 1) * per_pair))
            first = 3 * j * 128
            at = slice(j * 128, (j + 1) * 128)
            dqkv[:, first + 128 : first + 256] = dk[:, at].astype(BF16)
            dqkv[:, first + 256 : first + 384] = dv[:, at].astype(BF16)
            src = sum_w[j].src
            for b in range(width // 256):
                got = dot(n1[b * 256 : (b + 1) * 256, :], dqkv[:, first : first + 384]).astype(BF16)
                for n in range(256 // rows_w):
                    e = b * (256 // rows_w) + n
                    for m in range(3):
                        src[e % 2, e // 2, m] = got[n * rows_w : (n + 1) * rows_w, m * 128 : (m + 1) * 128]
            sum_w[j].start()
            if j > 0:
                sum_w[j - 1].spread()
        sum_w[pairs - 1].spread()
        sum_o.start()
        gather2.drain()
        red = Combine(p, xall, *g["red"][0:2], None, None, g["red"][2:4], (None, None), 1)
        for owner in range(n_seq):
            piece = dqkv[pl.ds(owner * tok, tok), :]
            xall[0, owner] = dot(piece, w_all[...], ((1,), (1,))).astype(BF16)
        red.start(0)
        sum_o.spread()
        d_sums = dot(jnp.ones((8, total), BF16), dqkv[...])
        for j in range(pairs):
            at = pl.ds(pl.multiple_of(p.s * cols + j * 128, 128), 128)
            first = 3 * j * 128
            vec_own[2:3, at] = d_sums[0:1, first : first + 128]
            vec_own[3:4, at] = d_sums[0:1, first + 256 : first + 384]
        sums = sum_w + [sum_o]
        ffn_pass(4, 5, 6, 7)
        sums[0].reduce()
        sums[0].forward(0)
        red.pass_on(0)
        for n in range(1, len(sums)):
            sums[n].reduce()
            sums[n].forward(0)
            sums[n - 1].relay(0)
        ffn_finish(4, 5, 6, 7)
        red.arrived(0)
        half_tok = tok // 2
        for n in range(2):
            gout[p.s, pl.ds(n * half_tok, half_tok), :] = red.summed(0, n).astype(BF16)

        def norm_one_back(n, carry):
            at = tile_rows(n)
            g_one = gout[p.s, at, :].astype(F32)
            _, xhat, inv_std = layer_norm(tok_ref[at, :].astype(F32), gain1, 0.0)
            gin_ref[at, :] += norm_back(g_one, xhat, inv_std, gain1)
            new = (g_one * xhat, g_one)
            return tuple(old + jnp.sum(v, axis=0, keepdims=True) for old, v in zip(carry, new))

        sums1 = lax.fori_loop(0, tok // tile, norm_one_back, (zero_row,) * 2)
        store_gin = pltpu.make_async_copy(gin_ref, gin_out, local_sems.at[0])
        store_gin.start()
        for n in range(2):
            vec_own[n : n + 1, :] = sums1[n]
        vec_seq[p.s] = vec_own[...]

        def tell(other):
            return p.to_seq(vec_own, vec_seq.at[p.s], r["vs_send"].at[other], r["vs_recv"].at[p.s], other)

        def told(other):
            return p.to_seq(vec_own, vec_seq.at[other], r["vs_send"].at[other], r["vs_recv"].at[other], other)

        others = (p.near, p.far, p.diag)
        for other in others:
            tell(other).start()
        for hop in range(1, chips):
            for one in sums:
                one.forward(hop)
                if hop > 1 or one is sums[-1]:
                    one.relay(hop - 1)
        for other in others:
            told(other).wait_recv()
        for other in others:
            tell(other).wait_send()
        vec = vec_seq[0]
        for n in range(1, n_seq):
            vec = vec + vec_seq[n]
        vec_own[...] = vec
        vec_exp[p.e] = vec

        def show(step):
            other = p.peer(step, -1)
            return p.to_exp(vec_own, vec_exp.at[p.e], r["ve_send"].at[step], r["ve_recv"].at[step], other)

        def shown(step):
            other = p.peer(step, 1)
            return p.to_exp(vec_own, vec_exp.at[other], r["ve_send"].at[step], r["ve_recv"].at[step], other)

        for step in range(1, n_exp):
            show(step).start()
        for one in sums:
            one.relay(chips - 1)
        comb_f.drain()
        out_ref = part.at[0]
        for n in range(tok // 128):
            at = slice(n * 128, (n + 1) * 128)
            rows_back = dot(pick[:, at], ret[...].reshape(n_exp * cap, width), ((0,), (0,)))
            out_ref[n * 128 // cap : (n + 1) * 128 // cap] = (
                (resid[at, :] + rows_back).astype(BF16).reshape(128 // cap, cap, width)
            )
        store_out = pltpu.make_async_copy(out_ref, out_out, local_sems.at[1])
        store_out.start()
        for hop in range(chips):
            for one in sums:
                one.arrived(hop)
        for step in range(1, n_exp):
            shown(step).wait_recv()
            show(step).wait_send()
        vec = vec_exp[0]
        for n in range(1, n_exp):
            vec = vec + vec_exp[n]
        vec_ref[...] = vec
        disp_c.drain()
        disp_n.drain(seq=False)
        for one in sums:
            one.drain()
        store_gin.wait()
        store_out.wait()

    vmem = pl.BlockSpec(memory_space=pltpu.VMEM)
    hbm = pl.BlockSpec(memory_space=pl.ANY)
    smem = pl.BlockSpec(memory_space=pltpu.SMEM)
    shape = jax.ShapeDtypeStruct
    return pl.pallas_call(
        kernel,
        out_shape=[
            shape((n_seq, cap, width), BF16),
            shape((tok, width), F32),
            shape((8, width), F32),
            shape((1, hidden), F32),
            shape((1, width), F32),
            shape((width, hidden), F32),
            shape((hidden, width), F32),
            shape((3, width, width), BF16),
            shape((width, width), BF16),
        ],
        in_specs=[vmem] * 3 + [smem] + [vmem] * 2 + [hbm] * 3 + [vmem] * 2 + [hbm] + [vmem] * 3
        + [hbm, vmem, hbm, vmem],
        out_specs=[hbm, hbm] + [vmem] * 3 + [hbm] * 4,
        scratch_shapes=scratch,
        compiler_params=pltpu.CompilerParams(
            collective_id=collective_id, has_side_effects=True, vmem_limit_bytes=VMEM_LIMIT
        ),
        name="layer",
    )(tokens, ids, cotangent, lengths, *ln1, *w_qkv, b_query, b_value, w_out, b_out, *ln2, w_up, b_up, w_down, b_down)


def finish(output, input_grad, vec, dbu, csum, dwu, dwd, gw, go):
    tok, width = output.shape
    hidden = dwu.shape[1]
    cols = width // 4
    piece = 256

    def kernel(out_in, gin_in, vec_ref, dbu_in, csum_ref, dwu_in, dwd_in, gw_in, go_in, *refs):
        (out_o, gin_o, l1g, l1b, wq_o, bq_o, wk_o, wv_o, bv_o, wo_o, bo_o, l2g, l2b, dwu_o, dbu_o, dwd_o, dbd_o) = refs[:17]
        small, wide, same_b, same_f, sems = refs[17:22]
        count = 0

        def pair(src, mid_in, mid_out, dst):
            nonlocal count
            load = pltpu.make_async_copy(src, mid_in, sems.at[count])
            store = pltpu.make_async_copy(mid_out, dst, sems.at[count + 1])
            count += 2
            return load, store

        widen, plain = [], []
        for m, (src, dst) in enumerate(
            ((gw_in.at[0], wq_o), (gw_in.at[1], wk_o), (gw_in.at[2], wv_o), (go_in, wo_o))
        ):
            for n in range(width // piece):
                rows = pl.ds(n * piece, piece)
                at = m * (width // piece) + n
                widen.append((pair(src.at[rows], small.at[at], wide.at[at], dst.at[rows]), at))
        at = 0
        for src, dst, total in ((dwu_in, dwu_o.at[0], width), (dwd_in, dwd_o.at[0], hidden), (gin_in, gin_o.at[0], tok)):
            for n in range(total // piece):
                rows = pl.ds(n * piece, piece)
                plain.append(pair(src.at[rows], same_f.at[at], same_f.at[at], dst.at[rows]))
                at += 1
        plain.append(pair(out_in, same_b, same_b, out_o.at[0]))
        order = []
        for n in range(max(len(widen), len(plain))):
            order += widen[n : n + 1] + [(c, None) for c in plain[n : n + 1]]
        for (load, _), _ in order:
            load.start()
        for n, ref in enumerate((l1g, l1b, bq_o, bv_o, bo_o, l2g, l2b)):
            ref[...] = vec_ref[n : n + 1, :].reshape(width)
        dbu_o[...] = dbu_in[...]
        first = pl.multiple_of(lax.axis_index("seq") * cols, cols)
        dbd_o[...] = csum_ref[:, pl.ds(first, cols)]
        for (load, store), at in order:
            load.wait()
            if at is not None:
                wide[at] = small[at].astype(F32)
            store.start()
        for (_, store), _ in order:
            store.wait()

    vmem = pl.BlockSpec(memory_space=pltpu.VMEM)
    hbm = pl.BlockSpec(memory_space=pl.ANY)
    shape = jax.ShapeDtypeStruct
    row, square = shape((width,), F32), shape((width, width), F32)
    n_widen = 4 * (width // piece)
    n_plain = (width + hidden + tok) // piece
    return pl.pallas_call(
        kernel,
        out_shape=[
            shape((1, tok, width), BF16), shape((1, tok, width), F32), row, row, square, row, square, square, row,
            square, row, row, row, shape((1, width, hidden), F32), shape((1, hidden), F32),
            shape((1, hidden, width), F32), shape((1, cols), F32),
        ],
        in_specs=[hbm, hbm, vmem, vmem, vmem, hbm, hbm, hbm, hbm],
        out_specs=[hbm, hbm, vmem, vmem, hbm, vmem, hbm, hbm, vmem, hbm, vmem, vmem, vmem, hbm, vmem, hbm, vmem],
        scratch_shapes=[
            pltpu.VMEM((n_widen, piece, width), BF16),
            pltpu.VMEM((n_widen, piece, width), F32),
            pltpu.VMEM((tok, width), BF16),
            pltpu.VMEM((n_plain, piece, width), F32),
            pltpu.SemaphoreType.DMA((2 * (n_widen + n_plain + 1),)),
        ],
        compiler_params=pltpu.CompilerParams(vmem_limit_bytes=VMEM_LIMIT),
        name="finish",
    )(output, input_grad, vec, dbu, csum, dwu, dwd, gw, go)


def shards(
    tokens, lengths, expert_ids, ln1_gain, ln1_bias, w_query, b_query, w_key, w_value, b_value, w_out, b_out,
    ln2_gain, ln2_bias, w_up, b_up, w_down, b_down, cotangent,
):
    output, *parts = layer(
        tokens[0], expert_ids[0, :, 0][None], cotangent[0], lengths, (ln1_gain, ln1_bias),
        (w_query, w_key, w_value), b_query, b_value, w_out, b_out, (ln2_gain, ln2_bias), w_up[0], b_up, w_down[0],
        b_down, lax.axis_size("exp"), 0,
    )
    return tuple(finish(output.reshape(tokens.shape[1:]), *parts))


def norm_layer(values_in, gain_vec, shift_vec):
    center = values_in - jnp.mean(values_in, axis=-1, keepdims=True)
    inv_std = lax.rsqrt(jnp.mean(center * center, axis=-1, keepdims=True) + EPSILON)
    return center * inv_std * gain_vec + shift_vec


def segment_ids(positions, seq_ends):
    return jnp.sum((positions[:, None] >= seq_ends[None, :]).astype(jnp.int32), axis=1)


def visible_pairs(query_pos, query_seg, key_pos, key_seg):
    return ((query_seg[:, None] == key_seg[None, :]) & (key_pos[None, :] <= query_pos[:, None]))[
        None
    ]


def project(left_op, right_op):
    return jnp.dot(left_op, right_op, preferred_element_type=jnp.float32)


def shards_any(
    tokens,
    lengths,
    expert_ids,
    ln1_gain,
    ln1_bias,
    w_query,
    b_query,
    w_key,
    w_value,
    b_value,
    w_out,
    b_out,
    ln2_gain,
    ln2_bias,
    w_up,
    b_up,
    w_down,
    b_down,
    cotangent,
):
    tok_rows = tokens.shape[1]
    width = tokens.shape[2]
    seq_size = lax.axis_size("seq")
    exp_size = lax.axis_size("exp")
    seq_rank = lax.axis_index("seq")
    seq_ends = jnp.cumsum(lengths[0])
    own_pos = seq_rank * tok_rows + jnp.arange(tok_rows, dtype=jnp.int32)
    own_seg = segment_ids(own_pos, seq_ends)
    inputs = tokens[0].astype(jnp.float32)
    gain_one = ln1_gain.astype(jnp.float32)
    bias_one = ln1_bias.astype(jnp.float32)
    gain_two = ln2_gain.astype(jnp.float32)
    bias_two = ln2_bias.astype(jnp.float32)
    normed_one_low = norm_layer(inputs, gain_one, bias_one).astype(jnp.bfloat16)
    query_low = (project(normed_one_low, w_query) + b_query.astype(jnp.float32)).astype(
        jnp.bfloat16
    )
    keys_low = project(normed_one_low, w_key).astype(jnp.bfloat16)
    values_low = (project(normed_one_low, w_value) + b_value.astype(jnp.float32)).astype(
        jnp.bfloat16
    )
    query_heads = query_low.reshape(tok_rows, HEADS, HEAD_DIM)
    initial = (
        jnp.full((HEADS, tok_rows), MASKED_SCORE, jnp.float32),
        jnp.zeros((HEADS, tok_rows), jnp.float32),
        jnp.zeros((HEADS, tok_rows, HEAD_DIM), jnp.float32),
    )
    key_piece = lax.all_gather(keys_low, "seq", axis=0, tiled=True)
    value_piece = lax.all_gather(values_low, "seq", axis=0, tiled=True)
    piece_len = key_piece.shape[0]
    fold_block_len = math.gcd(piece_len, 512)
    block_count = piece_len // fold_block_len
    key_blocks = key_piece.reshape(block_count, fold_block_len, HEADS, HEAD_DIM)
    value_blocks = value_piece.reshape(block_count, fold_block_len, HEADS, HEAD_DIM)
    offsets = jnp.arange(block_count, dtype=jnp.int32) * fold_block_len

    def block_step(state_now, packed):
        row_max, row_total, accumulated = state_now
        key_blk, value_blk, offset = packed
        key_pos = offset + jnp.arange(fold_block_len, dtype=jnp.int32)
        allowed = visible_pairs(own_pos, own_seg, key_pos, segment_ids(key_pos, seq_ends))
        scores = (
            jnp.einsum("qhd,khd->hqk", query_heads, key_blk, preferred_element_type=jnp.float32)
            * SCORE_SCALE
        )
        masked = jnp.where(allowed, scores, MASKED_SCORE)
        new_max = jnp.maximum(row_max, jnp.max(masked, axis=-1))
        weights = jnp.where(allowed, jnp.exp(masked - new_max[..., None]), 0.0)
        factor = jnp.exp(row_max - new_max)
        row_total = row_total * factor + jnp.sum(weights, axis=-1)
        accumulated = accumulated * factor[..., None] + jnp.einsum(
            "hqk,khd->hqd",
            weights.astype(jnp.bfloat16),
            value_blk,
            preferred_element_type=jnp.float32,
        )
        return ((new_max, row_total, accumulated), None)

    result, _ = lax.scan(block_step, initial, (key_blocks, value_blocks, offsets))
    row_max, row_total, accumulated = result
    attn_heads = accumulated / row_total[..., None]
    attn_low = jnp.transpose(attn_heads, (1, 0, 2)).reshape(tok_rows, width).astype(jnp.bfloat16)
    resid = inputs + project(attn_low, w_out) + b_out.astype(jnp.float32)
    normed_two_low = norm_layer(resid, gain_two, bias_two).astype(jnp.bfloat16)
    experts = exp_size * w_up.shape[0]
    capacity = 2 * tok_rows // experts
    expert_of = expert_ids[0, :, 0]
    onehot = (expert_of[:, None] == jnp.arange(experts, dtype=jnp.int32)[None, :]).astype(jnp.int32)
    slot_of = jnp.sum(onehot * (jnp.cumsum(onehot, axis=0) - onehot), axis=1)
    send_rows = (
        jnp.zeros((experts, capacity, width), jnp.bfloat16)
        .at[expert_of, slot_of]
        .set(normed_two_low)
    )
    received = lax.all_to_all(send_rows, "exp", split_axis=0, concat_axis=0, tiled=True)
    recv_count = experts * capacity
    recv_rows = received.reshape(recv_count, width)
    up_weight = w_up[0]
    up_bias = b_up[0]
    down_weight = w_down[0]
    down_bias = b_down[0].astype(jnp.float32)
    piece_width = width // seq_size
    grad_send = (
        jnp.zeros((experts, capacity, width), jnp.bfloat16).at[expert_of, slot_of].set(cotangent[0])
    )
    gathered = lax.all_gather(recv_rows, "seq", axis=0, tiled=True)
    preact = project(gathered, up_weight) + up_bias.astype(jnp.float32)
    act_low = jax.nn.gelu(preact).astype(jnp.bfloat16)
    part = act_low
    expert_out = (
        lax.psum_scatter(
            project(part, down_weight).astype(jnp.bfloat16), "seq", scatter_dimension=0, tiled=True
        ).astype(jnp.float32)
        + down_bias
    )
    returned = lax.all_to_all(
        expert_out.astype(jnp.bfloat16).reshape(experts, capacity, width),
        "exp",
        split_axis=0,
        concat_axis=0,
        tiled=True,
    )
    grad_recv = lax.all_to_all(grad_send, "exp", split_axis=0, concat_axis=0, tiled=True).reshape(
        recv_count, width
    )
    grad_all = lax.all_gather(grad_recv, "seq", axis=0, tiled=True)
    bias_full = jnp.sum(grad_all.astype(jnp.float32), axis=0)
    grad_b_down = lax.dynamic_slice_in_dim(bias_full, seq_rank * piece_width, piece_width, 0)
    grad_act = jnp.einsum("rd,fd->rf", grad_all, down_weight, preferred_element_type=jnp.float32)
    grad_pre = jax.vjp(jax.nn.gelu, preact)[1](grad_act)[0].astype(jnp.bfloat16)
    grad_w_down = jnp.einsum("rf,rd->fd", act_low, grad_all, preferred_element_type=jnp.float32)
    grad_w_up = jnp.einsum("rd,rf->df", gathered, grad_pre, preferred_element_type=jnp.float32)
    grad_b_up = jnp.sum(grad_pre.astype(jnp.float32), axis=0)
    part = grad_pre
    grad_home = lax.psum_scatter(
        jnp.einsum("rf,df->rd", part, up_weight, preferred_element_type=jnp.float32).astype(
            jnp.bfloat16
        ),
        "seq",
        scatter_dimension=0,
        tiled=True,
    )
    ffn_rows = returned[expert_of, slot_of].astype(jnp.float32)
    output = (resid + ffn_rows).astype(jnp.bfloat16)
    grad_back = lax.all_to_all(
        grad_home.reshape(experts, capacity, width), "exp", split_axis=0, concat_axis=0, tiled=True
    )
    grad_normed_two = grad_back[expert_of, slot_of].astype(jnp.float32)
    _, norm_two_back = jax.vjp(norm_layer, resid, gain_two, bias_two)
    grad_resid_norm, grad_gain_two, grad_bias_two = norm_two_back(grad_normed_two)
    grad_resid = cotangent[0].astype(jnp.float32) + grad_resid_norm
    grad_out_low = grad_resid.astype(jnp.bfloat16)
    grad_w_out = jnp.einsum("qa,qd->ad", attn_low, grad_out_low, preferred_element_type=jnp.float32)
    grad_b_out = jnp.sum(grad_out_low.astype(jnp.float32), axis=0)
    grad_attn_low = jnp.einsum(
        "qd,ad->qa", grad_out_low, w_out, preferred_element_type=jnp.float32
    ).astype(jnp.bfloat16)
    grad_attn_heads = grad_attn_low.reshape(tok_rows, HEADS, HEAD_DIM)
    delta = jnp.sum(
        jnp.transpose(grad_attn_heads.astype(jnp.float32), (1, 0, 2)) * attn_heads, axis=-1
    )
    whole_keys, whole_values = (
        lax.all_gather(keys_low, "seq", axis=0, tiled=True),
        lax.all_gather(values_low, "seq", axis=0, tiled=True),
    )
    group_len = whole_keys.shape[0]
    block_len = math.gcd(group_len, 512)
    block_count = group_len // block_len

    def back_step(grad_query, packed):
        key_blk, value_blk, offset = packed
        key_pos = offset + jnp.arange(block_len, dtype=jnp.int32)
        allowed = visible_pairs(own_pos, own_seg, key_pos, segment_ids(key_pos, seq_ends))
        scores = (
            jnp.einsum("qhd,khd->hqk", query_heads, key_blk, preferred_element_type=jnp.float32)
            * SCORE_SCALE
        )
        masked = jnp.where(allowed, scores, MASKED_SCORE)
        probabilities = (
            jnp.where(allowed, jnp.exp(masked - row_max[..., None]), 0.0) / row_total[..., None]
        )
        probs_low = probabilities.astype(jnp.bfloat16)
        grad_probs = jnp.einsum(
            "qhd,khd->hqk", grad_attn_heads, value_blk, preferred_element_type=jnp.float32
        )
        grad_scores = (probabilities * (grad_probs - delta[..., None])).astype(jnp.bfloat16)
        grad_query = (
            grad_query
            + jnp.einsum("hqk,khd->qhd", grad_scores, key_blk, preferred_element_type=jnp.float32)
            * SCORE_SCALE
        )
        grad_key_blk = (
            jnp.einsum("hqk,qhd->khd", grad_scores, query_heads, preferred_element_type=jnp.float32)
            * SCORE_SCALE
        )
        grad_value_blk = jnp.einsum(
            "hqk,qhd->khd", probs_low, grad_attn_heads, preferred_element_type=jnp.float32
        )
        return (grad_query, (grad_key_blk, grad_value_blk))

    block_offsets = jnp.arange(block_count, dtype=jnp.int32) * block_len
    grad_query, key_value_parts = lax.scan(
        back_step,
        jnp.zeros((tok_rows, HEADS, HEAD_DIM), jnp.float32),
        (
            whole_keys.reshape(block_count, block_len, HEADS, HEAD_DIM),
            whole_values.reshape(block_count, block_len, HEADS, HEAD_DIM),
            block_offsets,
        ),
    )
    grad_keys, grad_values = (
        lax.psum_scatter(
            key_value_parts[0].reshape(group_len, width).astype(jnp.bfloat16),
            "seq",
            scatter_dimension=0,
            tiled=True,
        ).astype(jnp.float32),
        lax.psum_scatter(
            key_value_parts[1].reshape(group_len, width).astype(jnp.bfloat16),
            "seq",
            scatter_dimension=0,
            tiled=True,
        ).astype(jnp.float32),
    )
    grad_query_low = grad_query.reshape(tok_rows, width).astype(jnp.bfloat16)
    grad_keys_low = grad_keys.astype(jnp.bfloat16)
    grad_values_low = grad_values.astype(jnp.bfloat16)
    grad_w_query = jnp.einsum(
        "qa,qd->ad", normed_one_low, grad_query_low, preferred_element_type=jnp.float32
    )
    grad_b_query = jnp.sum(grad_query_low.astype(jnp.float32), axis=0)
    grad_w_key = jnp.einsum(
        "qa,qd->ad", normed_one_low, grad_keys_low, preferred_element_type=jnp.float32
    )
    grad_w_value = jnp.einsum(
        "qa,qd->ad", normed_one_low, grad_values_low, preferred_element_type=jnp.float32
    )
    grad_b_value = jnp.sum(grad_values_low.astype(jnp.float32), axis=0)
    grad_normed_one = (
        (
            jnp.einsum("qd,ad->qa", grad_query_low, w_query, preferred_element_type=jnp.float32)
            + jnp.einsum("qd,ad->qa", grad_keys_low, w_key, preferred_element_type=jnp.float32)
            + jnp.einsum("qd,ad->qa", grad_values_low, w_value, preferred_element_type=jnp.float32)
        )
        .astype(jnp.bfloat16)
        .astype(jnp.float32)
    )
    _, norm_one_back = jax.vjp(norm_layer, inputs, gain_one, bias_one)
    grad_in_norm, grad_gain_one, grad_bias_one = norm_one_back(grad_normed_one)
    input_grad = grad_resid + grad_in_norm
    summed = lax.psum(
        (
            grad_gain_one,
            grad_bias_one,
            grad_w_query,
            grad_b_query,
            grad_w_key,
            grad_w_value,
            grad_b_value,
            grad_w_out,
            grad_b_out,
            grad_gain_two,
            grad_bias_two,
        ),
        ("seq", "exp"),
    )
    return (
        output[None],
        input_grad[None],
        summed[0],
        summed[1],
        summed[2],
        summed[3],
        summed[4],
        summed[5],
        summed[6],
        summed[7],
        summed[8],
        summed[9],
        summed[10],
        grad_w_up[None],
        grad_b_up[None],
        grad_w_down[None],
        grad_b_down[None],
    )


def solution(mesh):
    placed = (
        P("exp", "seq", None),
        P("exp", None),
        P("exp", "seq", None),
        P(),
        P(),
        P(),
        P(),
        P(),
        P(),
        P(),
        P(),
        P(),
        P(),
        P(),
        P("exp", None, "seq"),
        P("exp", "seq"),
        P("exp", "seq", None),
        P("exp", None),
        P("exp", "seq", None),
    )
    plane = mesh.shape["seq"] == 4 and mesh.shape["exp"] == 8
    return jax.shard_map(
        shards if plane else shards_any,
        mesh=mesh,
        in_specs=placed,
        out_specs=(
            P("exp", "seq", None),
            P("exp", "seq", None),
            P(),
            P(),
            P(),
            P(),
            P(),
            P(),
            P(),
            P(),
            P(),
            P(),
            P(),
            P("exp", None, "seq"),
            P("exp", "seq"),
            P("exp", "seq", None),
            P("exp", "seq"),
        ),
        check_vma=False,
    )
```

profile of v0, /device:TPU:25, one launch (start us, length us, event | category | flops | bytes accessed | tf_op | source)
XLA Modules:
  0.0 290.1 jit_solution(4848922209542618544)
XLA Ops:
  0.7 272.3 %layer.1 = (bf16[4,64,1024]{2,1,0:T(8,128)(2,1)}, f32[256,1024]{1,0:T(8,128)}, f32[8,1024]{1,0:T(8,128)}, f32[1,1024]{1,0:T(1,128)}, f32[1,1024]{1,0:T(1,128)}, ...) custom-call(bf16[256,1024]{1,0:T(8,128)(2,1)} %bitcast.8, ...), custom_call_target="tpu_custom_call" | custom-call | tf_op jit(solution)/shard_map/layer/pallas_call | solution.py:1153
  273.0 16.9 %finish.1 = (bf16[1,256,1024]{2,1,0:T(8,128)(2,1)}, f32[1,256,1024]{2,1,0:T(8,128)}, f32[1024]{0:T(1024)}, f32[1024]{0:T(1024)}, f32[1024,1024]{1,0:T(8,128)}, /...) custom-call(bf16[256,1024]{1,0:T(8,128)(2,1)} %bitcast.10, ...), custom_call_target="tpu_custom_call" | custom-call | tf_op jit(solution)/shard_map/finish/pallas_call | solution.py:1234
where the time goes:
time: 292 us; the launch traced here: 290 us
  Pallas kernels  289 us (99%)
    pallas_call x1, Pallas kernels, layer(): pl.pallas_call(kernel, out_shape=[shape((n_seq, cap, width), BF16), shape...  272 us
    pallas_call x1, Pallas kernels, finish(): pl.pallas_call(kernel, out_shape=[shape((1, tok, width), BF16), shape((1,...  16.9 us

commit v1 on v0

--- a/solution.py
+++ b/solution.py
@@ -906,9 +906,7 @@
             return carry
 
         lax.fori_loop(1, n_exp + 4, loop, 0)
-        ffn_pass(0, 1)
         comb_g.drain()
-        ffn_pass(2, 3)
 
         for c in stores:
             c.wait()
@@ -952,6 +950,10 @@
                 per_head, g_rows.astype(F32) * attn[rows, :], (((1,), (1,)), ((), ())),
                 precision=lax.Precision.HIGHEST, preferred_element_type=F32,
             )
+            masks = [head_mask(tok, cols, head) for head in some_heads]
+            zero = jnp.zeros_like(q_rows)
+            q_owns = [jnp.where(own, q_rows, zero) for own in masks]
+            g_owns = [jnp.where(own, g_rows, zero) for own in masks]
             dq[...] = jnp.zeros_like(dq)
 
             def key_block(n, carry):
@@ -962,10 +964,7 @@
                 dq_new = jnp.zeros((tok, cols), F32)
                 dk_new = jnp.zeros((tok, cols), F32)
                 dv_new = jnp.zeros((tok, cols), F32)
-                for head in some_heads:
-                    own = head_mask(tok, cols, head)
-                    q_own = jnp.where(own, q_rows, jnp.zeros_like(q_rows))
-                    g_own = jnp.where(own, g_rows, jnp.zeros_like(g_rows))
+                for head, own, q_own, g_own in zip(some_heads, masks, q_owns, g_owns):
                     scores = dot(k_rows, q_own, ((1,), (1,)))
                     probs = jnp.where(allowed, jnp.exp(scores - lse_all[head : head + 1, rows]), 0.0)
                     g_probs = dot(v_rows, g_own, ((1,), (1,)))
@@ -986,13 +985,14 @@
         every = range(heads)
         grad_attn(p.s)
         gather2.relay()
+        ffn_pass(0, 1, 2, 3)
         attn_back(p.s, every)
-        ffn_finish(0, 1, 2, 3)
         gather2.wait((2, 3))
         grad_attn(p.near)
         attn_back(p.near, every)
         grad_attn(p.far)
         attn_back(p.far, every)
+        ffn_finish(0, 1, 2, 3)
         gather2.wait((4, 5))
         ffn_start(4, 5, 6, 7)
         grad_attn(p.diag)
@@ -1022,6 +1022,7 @@
             for n in range(128 // rows_o):
                 e = b * (128 // rows_o) + n
                 sum_o.src[e % 2, e // 2] = got[n * rows_o : (n + 1) * rows_o]
+        sum_o.start()
         for j in range(pairs):
             attn_back(p.diag, range(j * per_pair, (j + 1) * per_pair))
             first = 3 * j * 128
@@ -1036,33 +1037,32 @@
                     for m in range(3):
                         src[e % 2, e // 2, m] = got[n * rows_w : (n + 1) * rows_w, m * 128 : (m + 1) * 128]
             sum_w[j].start()
+            if j == 0:
+                sum_o.spread()
             if j > 0:
                 sum_w[j - 1].spread()
+        sum_o.reduce()
+        sum_o.forward(0)
         sum_w[pairs - 1].spread()
-        sum_o.start()
         gather2.drain()
         red = Combine(p, xall, *g["red"][0:2], None, None, g["red"][2:4], (None, None), 1)
         for owner in range(n_seq):
             piece = dqkv[pl.ds(owner * tok, tok), :]
             xall[0, owner] = dot(piece, w_all[...], ((1,), (1,))).astype(BF16)
         red.start(0)
-        sum_o.spread()
         d_sums = dot(jnp.ones((8, total), BF16), dqkv[...])
         for j in range(pairs):
             at = pl.ds(pl.multiple_of(p.s * cols + j * 128, 128), 128)
             first = 3 * j * 128
             vec_own[2:3, at] = d_sums[0:1, first : first + 128]
             vec_own[3:4, at] = d_sums[0:1, first + 256 : first + 384]
-        sums = sum_w + [sum_o]
+        sums = [sum_o] + sum_w
         ffn_pass(4, 5, 6, 7)
-        sums[0].reduce()
-        sums[0].forward(0)
         red.pass_on(0)
         for n in range(1, len(sums)):
             sums[n].reduce()
             sums[n].forward(0)
             sums[n - 1].relay(0)
-        ffn_finish(4, 5, 6, 7)
         red.arrived(0)
         half_tok = tok // 2
         for n in range(2):
@@ -1093,6 +1093,7 @@
         for other in others:
             tell(other).start()
         for hop in range(1, chips):
+            ffn_finish(*range(4 + 4 * (hop - 1) // (chips - 1), 4 + 4 * hop // (chips - 1)))
             for one in sums:
                 one.forward(hop)
                 if hop > 1 or one is sums[-1]:

time: 292 us -> 286 us (0.979)
  Pallas kernels: 289 us -> 284 us
    pallas_call x1, Pallas kernels: 272 us -> 267 us  [layer(): pl.pallas_call(kernel, out_shape=[shape((n_seq, cap, width), BF16), shape...]
where the time goes in v1:
time: 286 us; the launch traced here: 285 us
  Pallas kernels  284 us (99%)
    pallas_call x1, Pallas kernels, layer(): pl.pallas_call(kernel, out_shape=[shape((n_seq, cap, width), BF16), shape...  267 us
    pallas_call x1, Pallas kernels, finish(): pl.pallas_call(kernel, out_shape=[shape((1, tok, width), BF16), shape((1,...  16.9 us

profile of v1, /device:TPU:25, one launch (start us, length us, event | category | flops | bytes accessed | tf_op | source)
XLA Modules:
  0.0 285.0 jit_solution(10739521763318839435)
XLA Ops:
  0.7 267.3 %layer.1 = (bf16[4,64,1024]{2,1,0:T(8,128)(2,1)}, f32[256,1024]{1,0:T(8,128)}, f32[8,1024]{1,0:T(8,128)}, f32[1,1024]{1,0:T(1,128)}, f32[1,1024]{1,0:T(1,128)}, ...) custom-call(bf16[256,1024]{1,0:T(8,128)(2,1)} %bitcast.8, ...), custom_call_target="tpu_custom_call" | custom-call | tf_op jit(solution)/shard_map/layer/pallas_call | solution.py:1154
  267.9 16.9 %finish.1 = (bf16[1,256,1024]{2,1,0:T(8,128)(2,1)}, f32[1,256,1024]{2,1,0:T(8,128)}, f32[1024]{0:T(1024)}, f32[1024]{0:T(1024)}, f32[1024,1024]{1,0:T(8,128)}, /...) custom-call(bf16[256,1024]{1,0:T(8,128)(2,1)} %bitcast.10, ...), custom_call_target="tpu_custom_call" | custom-call | tf_op jit(solution)/shard_map/finish/pallas_call | solution.py:1235

commit v2 on v1

--- a/solution.py
+++ b/solution.py
@@ -821,12 +821,14 @@
             for step in steps:
                 comb_f.finish(step, bias_down)
 
+        disp_c.drain(seq=False)
+        keep_act, keep_grad = send_c.at[0:n_seq], send_c.at[n_seq : 2 * n_seq]
+
         def compute(step):
             x = held[step].reshape(routed, width)
             gr = cot[step].reshape(routed, width)
             ones = jnp.ones((8, routed), BF16)
             csum_ref[...] += dot(ones, gr)[0:1, :]
-            y = jnp.zeros((routed, width), F32)
             gx = jnp.zeros((routed, width), F32)
             for b in range(hidden // block):
                 at = pl.ds(b * block, block)
@@ -836,15 +838,22 @@
                 sq = pre * pre
                 th = jnp.tanh(GELU_A * pre * (1.0 + GELU_B * sq))
                 half = 0.5 * (1.0 + th)
-                act = (pre * half).astype(BF16)
                 slope = half + 0.5 * pre * (1.0 - th * th) * (GELU_A * (1.0 + 3.0 * GELU_B * sq))
                 g_pre = (g_act * slope).astype(BF16)
+                keep_act[:, :, at] = (pre * half).astype(BF16).reshape(n_seq, cap, block)
+                keep_grad[:, :, at] = g_pre.reshape(n_seq, cap, block)
+                gx = gx + dot(g_pre, wu_b, ((1,), (1,)))
+            part[lax.rem(step, slots)] = gx.astype(BF16).reshape(n_seq, cap, width)
+            comb_g.start(step)
+            y = jnp.zeros((routed, width), F32)
+            for b in range(hidden // block):
+                at = pl.ds(b * block, block)
+                act = keep_act[:, :, at].reshape(routed, block)
+                g_pre = keep_grad[:, :, at].reshape(routed, block)
                 dbu_ref[:, at] += dot(ones, g_pre)[0:1, :]
-                y = y + dot(act, wd_b)
-                gx = gx + dot(g_pre, wu_b, ((1,), (1,)))
+                y = y + dot(act, wd[at, :])
                 dwu[:, at] += dot(x, g_pre, ((0,), (0,)))
                 dwd[at, :] += dot(act, gr, ((0,), (0,)))
-            part[lax.rem(step, slots)] = gx.astype(BF16).reshape(n_seq, cap, width)
             disp_n.sent(step)
             held[step] = y.astype(BF16).reshape(n_seq, cap, width)
 
@@ -887,7 +896,6 @@
                 disp_c.arrived(t - 2)
                 disp_n.arrived(t - 2)
                 compute(t - 2)
-                comb_g.start(t - 2)
 
             @pl.when(t == n_exp + 1)
             def _():
@@ -1041,9 +1049,9 @@
                 sum_o.spread()
             if j > 0:
                 sum_w[j - 1].spread()
+        sum_w[pairs - 1].spread()
         sum_o.reduce()
         sum_o.forward(0)
-        sum_w[pairs - 1].spread()
         gather2.drain()
         red = Combine(p, xall, *g["red"][0:2], None, None, g["red"][2:4], (None, None), 1)
         for owner in range(n_seq):
@@ -1098,6 +1106,9 @@
                 one.forward(hop)
                 if hop > 1 or one is sums[-1]:
                     one.relay(hop - 1)
+            if hop > 1:
+                for one in sums:
+                    one.arrived(hop - 2)
         for other in others:
             told(other).wait_recv()
         for other in others:
@@ -1130,7 +1141,7 @@
             )
         store_out = pltpu.make_async_copy(out_ref, out_out, local_sems.at[1])
         store_out.start()
-        for hop in range(chips):
+        for hop in range(chips - 2, chips):
             for one in sums:
                 one.arrived(hop)
         for step in range(1, n_exp):
@@ -1140,7 +1151,8 @@
         for n in range(1, n_exp):
             vec = vec + vec_exp[n]
         vec_ref[...] = vec
-        disp_c.drain()
+        for step in range(n_exp):
+            disp_c.sent(step)
         disp_n.drain(seq=False)
         for one in sums:
             one.drain()

time: 286 us -> 279 us (0.976)
  Pallas kernels: 284 us -> 278 us
    pallas_call x1, Pallas kernels: 267 us -> 261 us  [layer(): pl.pallas_call(kernel, out_shape=[shape((n_seq, cap, width), BF16), shape...]
where the time goes in v2:
time: 279 us
  Pallas kernels  278 us (100%)
    pallas_call x1, Pallas kernels, layer(): pl.pallas_call(kernel, out_shape=[shape((n_seq, cap, width), BF16), shape...  261 us
    pallas_call x1, Pallas kernels, finish(): pl.pallas_call(kernel, out_shape=[shape((1, tok, width), BF16), shape((1,...  16.9 us

profile of v2, /device:TPU:25, one launch (start us, length us, event | category | flops | bytes accessed | tf_op | source)
XLA Modules:
  0.0 279.0 jit_solution(17891677420720282269)
XLA Ops:
  0.7 261.2 %layer.1 = (bf16[4,64,1024]{2,1,0:T(8,128)(2,1)}, f32[256,1024]{1,0:T(8,128)}, f32[8,1024]{1,0:T(8,128)}, f32[1,1024]{1,0:T(1,128)}, f32[1,1024]{1,0:T(1,128)}, ...) custom-call(bf16[256,1024]{1,0:T(8,128)(2,1)} %bitcast.8, ...), custom_call_target="tpu_custom_call" | custom-call | tf_op jit(solution)/shard_map/layer/pallas_call | solution.py:1166
  261.9 16.9 %finish.1 = (bf16[1,256,1024]{2,1,0:T(8,128)(2,1)}, f32[1,256,1024]{2,1,0:T(8,128)}, f32[1024]{0:T(1024)}, f32[1024]{0:T(1024)}, f32[1024,1024]{1,0:T(8,128)}, /...) custom-call(bf16[256,1024]{1,0:T(8,128)(2,1)} %bitcast.10, ...), custom_call_target="tpu_custom_call" | custom-call | tf_op jit(solution)/shard_map/finish/pallas_call | solution.py:1247

commit v3 on v2

--- a/solution.py
+++ b/solution.py
@@ -1071,6 +1071,7 @@
             sums[n].reduce()
             sums[n].forward(0)
             sums[n - 1].relay(0)
+        sum_o.forward(1)
         red.arrived(0)
         half_tok = tok // 2
         for n in range(2):
@@ -1089,6 +1090,8 @@
         store_gin.start()
         for n in range(2):
             vec_own[n : n + 1, :] = sums1[n]
+        for one in sum_w:
+            one.forward(1)
         vec_seq[p.s] = vec_own[...]
 
         def tell(other):
@@ -1103,7 +1106,8 @@
         for hop in range(1, chips):
             ffn_finish(*range(4 + 4 * (hop - 1) // (chips - 1), 4 + 4 * hop // (chips - 1)))
             for one in sums:
-                one.forward(hop)
+                if hop > 1:
+                    one.forward(hop)
                 if hop > 1 or one is sums[-1]:
                     one.relay(hop - 1)
             if hop > 1:

time: 279 us -> 279 us (level)
  no operation moved by 1% of the time
where the time goes in v3:
time: 279 us
  Pallas kernels  278 us (100%)
    pallas_call x1, Pallas kernels, layer(): pl.pallas_call(kernel, out_shape=[shape((n_seq, cap, width), BF16), shape...  261 us
    pallas_call x1, Pallas kernels, finish(): pl.pallas_call(kernel, out_shape=[shape((1, tok, width), BF16), shape((1,...  16.9 us

profile of v3, /device:TPU:25, one launch (start us, length us, event | category | flops | bytes accessed | tf_op | source)
XLA Modules:
  0.0 279.0 jit_solution(13421967792615831447)
XLA Ops:
  0.7 261.2 %layer.1 = (bf16[4,64,1024]{2,1,0:T(8,128)(2,1)}, f32[256,1024]{1,0:T(8,128)}, f32[8,1024]{1,0:T(8,128)}, f32[1,1024]{1,0:T(1,128)}, f32[1,1024]{1,0:T(1,128)}, ...) custom-call(bf16[256,1024]{1,0:T(8,128)(2,1)} %bitcast.8, ...), custom_call_target="tpu_custom_call" | custom-call | tf_op jit(solution)/shard_map/layer/pallas_call | solution.py:1170
  261.9 16.9 %finish.1 = (bf16[1,256,1024]{2,1,0:T(8,128)(2,1)}, f32[1,256,1024]{2,1,0:T(8,128)}, f32[1024]{0:T(1024)}, f32[1024]{0:T(1024)}, f32[1024,1024]{1,0:T(8,128)}, /...) custom-call(bf16[256,1024]{1,0:T(8,128)(2,1)} %bitcast.10, ...), custom_call_target="tpu_custom_call" | custom-call | tf_op jit(solution)/shard_map/finish/pallas_call | solution.py:1251
